TPU v7x, 256 devices: a whole 4x4x8 slice. The times are simulated.
256 devices in a mesh: row: 16 (over z, core), col: 16 (over x, y).
Axes of the slice: x: 4, y: 4, z: 8, core: 2. Of those that a mesh axis runs over, the one named last changes fastest.
Arguments:
- matrix: bfloat16 [2, 16, 256, 22, 16, 256], P(None, 'row', None, None, 'col'), as said below
Outputs:
- factored: bfloat16 [2, 16, 256, 22, 16, 256], P(None, 'row', None, None, 'col')
Inputs may be any that keep to these rules, and one draw needn't show every extreme that they name: `matrix`: every diagonal entry of the strip is twice or more the typical size of the sum of the off-diagonal entries in its row of its block, so that factoring without pivoting is stable.
All inputs are finite; a program needn't handle non-finite values.
Results may differ from a plain program's by a relative error of at most 0.0054.
Values may be sent and summed in bfloat16 or wider, within the bound.
A program may use at most 192 MiB of HBM per device.

v0:
```python
import jax, jax.numpy as jnp
from jax import lax
from jax.experimental import pallas as pl
from jax.experimental.pallas import tpu as pltpu
from jax.sharding import PartitionSpec as P

NB = 256
HB = 128
BF = jnp.bfloat16
F32 = jnp.float32


def dot32(a, b):
    return jnp.dot(a, b, precision=lax.Precision.HIGHEST, preferred_element_type=F32)


def dot16(a, b):
    return jnp.dot(a, b, preferred_element_type=F32)


def pick_lane(x, lane):
    return jnp.take_along_axis(x, jnp.full(x.shape, lane, jnp.int32), axis=1)


def pick_row(x, row):
    return jnp.broadcast_to(x[row : row + 1, :], x.shape)


def eliminate(m, rows, cols):
    lane = lax.broadcasted_iota(jnp.int32, (8, HB), 1)
    sub = lax.broadcasted_iota(jnp.int32, (8, HB), 0)

    def group(g, carry):
        base = pl.multiple_of(g * 8, 8)
        own = m[pl.ds(base, 8), :]
        cb = [pick_lane(own, base + u) for u in range(8)]
        saved_row = jnp.zeros((8, HB), F32)
        saved_col = cols[pl.ds(base, 8), :]
        for t in range(8):
            here = lane == base + t
            at = sub == t
            inv = 1.0 / pick_row(cb[t], t)
            saved_row = jnp.where(at, own, saved_row)
            saved_col = jnp.where(here, jnp.where(at, inv, cb[t] * inv), saved_col)
            mult = jnp.where(at, -1.0, cb[t])
            scaled = jnp.where(here, 1.0, pick_row(own, t)) * inv
            own = jnp.where(here | at, 0.0, own) - mult * scaled
            for u in range(t + 1, 8):
                cb[u] = jnp.where(at, 0.0, cb[u]) - mult * (pick_row(cb[u], t) * inv)
        inside = (lane >= base) & (lane < base + 8)
        wr = [pick_row(own, u) for u in range(8)]
        for r in range(HB // 8):
            part = pl.ds(8 * r, 8)
            old = m[part, :]
            cols[part, :] = jnp.where(inside, old, cols[part, :])
            new = jnp.where(inside, 0.0, old)
            for u in range(8):
                new = new - pick_lane(old, base + u) * wr[u]
            m[part, :] = new
        m[pl.ds(base, 8), :] = own
        rows[pl.ds(base, 8), :] = saved_row
        cols[pl.ds(base, 8), :] = saved_col
        return carry

    lax.fori_loop(0, HB // 8, group, 0)


def pieces(m, rows, cols):
    i = lax.broadcasted_iota(jnp.int32, (HB, HB), 0)
    j = lax.broadcasted_iota(jnp.int32, (HB, HB), 1)
    near = (i // 8) == (j // 8)
    c = cols[...]
    r = rows[...]
    small = jnp.where(near & (i < j), -c, jnp.where(i == j, c, 0.0))
    far = dot32(jnp.where(near, 0.0, c), small)
    mixed = jnp.where(near, c, far)
    low = jnp.where(i > j, mixed, 0.0)
    upinv = jnp.where(i < j, -mixed, jnp.where(i == j, c, 0.0))
    lowinv = jnp.where(i > j, r, jnp.where(i == j, 1.0, 0.0))
    packed = jnp.where(i > j, low, r)
    return m[...], packed, lowinv, upinv


def factor(a, linv, uinv, packed, m, rows, cols, keep):
    lo, hi = pl.ds(0, HB), pl.ds(HB, HB)
    m[...] = a[lo, lo]
    eliminate(m, rows, cols)
    inv, pk, li, ui = pieces(m, rows, cols)
    a12, a21 = a[lo, hi], a[hi, lo]
    w = dot32(inv, a12)
    m[...] = a[hi, hi] - dot32(a21, w)
    keep[0] = w
    keep[1] = dot32(a21, inv)
    packed[lo, lo] = pk.astype(BF)
    packed[lo, hi] = dot32(li, a12).astype(BF)
    packed[hi, lo] = dot32(a21, ui).astype(BF)
    linv[lo, lo] = li.astype(BF)
    uinv[lo, lo] = ui.astype(BF)
    eliminate(m, rows, cols)
    inv, pk, li, ui = pieces(m, rows, cols)
    packed[hi, hi] = pk.astype(BF)
    linv[hi, hi] = li.astype(BF)
    uinv[hi, hi] = ui.astype(BF)
    linv[hi, lo] = (-dot32(li, keep[1])).astype(BF)
    uinv[lo, hi] = (-dot32(keep[0], ui)).astype(BF)
    linv[lo, hi] = jnp.zeros((HB, HB), BF)
    uinv[hi, lo] = jnp.zeros((HB, HB), BF)

MESH = pl.DeviceIdType.MESH
NCOL = 22
PER = 2
NCH = NCOL * PER
CH = NB // PER


def comm(work, ring, corner, panel, rs, rr, ss, sr, ps, pr, ks, kr, loc):
    row = lax.axis_index("row")
    col = lax.axis_index("col")
    z, core = row // 2, row % 2
    x, y = col // 4, col % 4
    way = 1 - 2 * core
    dist = (z * way + 8) % 8
    nxt = ((z + way + 8) % 8) * 2 + core
    prv = ((z - way + 8) % 8) * 2 + core
    sib = row + way

    def at(xx, yy):
        return ((xx + 4) % 4) * 4 + (yy + 4) % 4

    barrier = pltpu.get_barrier_semaphore()
    for dev in (
        (nxt, col), (prv, col), (sib, col),
        (row, at(x + 1, y)), (row, at(x - 1, y)), (row, at(x, y + 1)), (row, at(x, y - 1)),
    ):
        pl.semaphore_signal(barrier, inc=1, device_id=dev, device_id_type=MESH)
    pl.semaphore_wait(barrier, 7)

    def piece(ref, n):
        return ref.at[n // PER, pl.ds(pl.multiple_of((n % PER) * CH, CH), CH), :]

    def remote(src, dst, send, recv, dev):
        return pltpu.make_async_remote_copy(
            src_ref=src, dst_ref=dst, send_sem=send, recv_sem=recv, device_id=dev, device_id_type=MESH
        )

    def ahead(n, src):
        return remote(piece(src, n), piece(ring.at[core], n), rs.at[n], rr.at[n], (nxt, col))

    def across(n, src):
        return remote(piece(src, n), piece(ring.at[core], n), ss.at[n], sr.at[n], (sib, col))

    mine = work.at[0]
    fill = pltpu.make_async_copy(mine, ring.at[core], loc.at[0])

    @pl.when(dist == 0)
    def _():
        fill.start()

    def step(n):
        @pl.when(dist == 0)
        def _():
            ahead(n, mine).start()
            across(n, mine).start()

        @pl.when(dist > 0)
        def _():
            ahead(n, ring.at[core]).wait_recv()

            @pl.when(dist < 7)
            def _():
                ahead(n, ring.at[core]).start()

            across(n, ring.at[core]).start()

    def steps(first, last):
        lax.fori_loop(first, last, lambda n, c: (step(n), c)[1], 0)

    def item(s, q):
        return corner.at[core, s] if q == 0 else panel.at[s, q - 1]

    def hop(s, q, slot, src, dev):
        return remote(src, item(s, q), ps.at[s, q, slot], pr.at[s, q], (row, dev))

    rel = [(y - s + 4) % 4 for s in range(2)]
    children = [
        lambda s: ((x == 0) & (rel[s] < 2), at(x, y + 1)),
        lambda s: ((x == 0) & (rel[s] == 0), at(x, y - 1)),
        lambda s: (x < 2, at(x + 1, y)),
        lambda s: (x == 0, at(x - 1, y)),
    ]

    def is_root(s):
        return (x == 0) & (rel[s] == 0)

    def spread(s, q, src):
        for slot, child in enumerate(children):
            cond, dev = child(s)

            @pl.when(cond)
            def _(slot=slot, dev=dev):
                hop(s, q, slot, src, dev).start()

    def twin(s, src):
        return remote(src, corner.at[core, s], ks.at[s], kr.at[s], (sib, col))

    def own(s, q, src):
        return pltpu.make_async_copy(src, item(s, q), loc.at[1 + s * 3 + q])

    def send(s, q, src):
        own(s, q, src).start()
        spread(s, q, src)
        if q == 0:
            twin(s, src).start()

    def relay(s, q):
        @pl.when(jnp.logical_not(is_root(s)))
        def _():
            hop(s, q, 0, item(s, q), col).wait_recv()
            spread(s, q, item(s, q))
            if q == 0:
                twin(s, item(s, q)).start()

    steps(0, PER)
    for s in range(2):
        @pl.when(is_root(s) & (dist == 0))
        def _(s=s):
            send(s, 0, mine.at[0])

        @pl.when(is_root(s) & (dist > 0))
        def _(s=s):
            send(s, 0, ring.at[core, 0])

        @pl.when(is_root(s))
        def _(s=s):
            for k in range(2):
                send(s, 1 + k, work.at[k, 0])

    steps(PER, PER + 4)
    for s in range(2):
        relay(s, 0)
    steps(PER + 4, PER + 12)
    for s in range(2):
        for k in range(2):
            relay(s, 1 + k)
    steps(PER + 12, NCH)

    @pl.when(dist == 0)
    def _():
        fill.wait()

    def drain(n, c):
        @pl.when(dist < 7)
        def _():
            ahead(n, ring.at[core]).wait_send()

        across(n, ring.at[core]).wait_send()
        other = piece(ring.at[1 - core], n)
        remote(other, other, ss.at[n], sr.at[n], (sib, col)).wait_recv()
        return c

    lax.fori_loop(0, NCH, drain, 0)
    for s in range(2):
        twin(s, corner.at[core, s]).wait_send()
        remote(corner.at[1 - core, s], corner.at[1 - core, s], ks.at[s], kr.at[s], (sib, col)).wait_recv()
        for q in range(3):
            for slot, child in enumerate(children):
                cond, dev = child(s)

                @pl.when(cond)
                def _(s=s, q=q, slot=slot, dev=dev):
                    hop(s, q, slot, item(s, q), dev).wait_send()

            @pl.when(is_root(s))
            def _(s=s, q=q):
                own(s, q, item(s, q)).wait()


def gather(work):
    block = jax.ShapeDtypeStruct
    hbm = pl.BlockSpec(memory_space=pl.ANY)
    dma = pltpu.SemaphoreType.DMA
    return pl.pallas_call(
        comm,
        out_shape=(
            block((2, NCOL, NB, NB), BF),
            block((2, 2, NB, NB), BF),
            block((2, 2, NB, NB), BF),
        ),
        in_specs=[hbm],
        out_specs=(hbm, hbm, hbm),
        scratch_shapes=[
            dma((NCH,)), dma((NCH,)), dma((NCH,)), dma((NCH,)),
            dma((2, 3, 4)), dma((2, 3)), dma((2,)), dma((2,)), dma((7,)),
        ],
        compiler_params=pltpu.CompilerParams(collective_id=0, has_side_effects=True),
        name="gather",
    )(work)


def small(corner, panel, linv, low, pan, packed, a, uinv, keep, urow, m, rows, cols, part):
    row = lax.axis_index("row")

    def solve_panel(s, k, block):
        keep_it = (k * 16 + row) > s
        out = dot16(block, uinv[...]).astype(BF)
        pan[s, k] = jnp.where(keep_it, out, jnp.zeros_like(out))

    a[...] = corner[0, 0].astype(F32)
    factor(a, linv.at[0], uinv, packed.at[0], m, rows, cols, part)
    for k in range(2):
        solve_panel(0, k, panel[0, k])
    low[...] = dot16(corner[1, 0], uinv[...]).astype(BF)
    urow[...] = dot16(linv[0], corner[0, 1]).astype(BF)
    a[...] = (corner[1, 1].astype(F32) - dot16(low[...], urow[...])).astype(BF).astype(F32)
    factor(a, linv.at[1], uinv, packed.at[1], m, rows, cols, part)
    for k in range(2):
        block = (panel[1, k].astype(F32) - dot16(pan[0, k], urow[...])).astype(BF)
        solve_panel(1, k, block)


def factors(corner, panel):
    block = jax.ShapeDtypeStruct
    vm = pl.BlockSpec(memory_space=pltpu.VMEM)
    return pl.pallas_call(
        small,
        out_shape=(
            block((2, NB, NB), BF),
            block((NB, NB), BF),
            block((2, 2, NB, NB), BF),
            block((2, NB, NB), BF),
        ),
        in_specs=[vm] * 2,
        out_specs=(vm,) * 4,
        scratch_shapes=[
            pltpu.VMEM((NB, NB), F32),
            pltpu.VMEM((NB, NB), BF),
            pltpu.VMEM((NB, NB), BF),
            pltpu.VMEM((NB, NB), BF),
            pltpu.VMEM((HB, HB), F32),
            pltpu.VMEM((HB, HB), F32),
            pltpu.VMEM((HB, HB), F32),
            pltpu.VMEM((2, HB, HB), F32),
        ],
        name="factors",
    )(corner, panel)


def bulk(work, ring, linv, low, pan, packed, out):
    row = lax.axis_index("row")
    col = lax.axis_index("col")
    j = pl.program_id(0)
    for b in range(WIDE):
        jj = j * WIDE + b
        cblk = jj * 16 + col
        u0 = dot16(linv[0], ring[0, b]).astype(BF)
        u0 = jnp.where(cblk > 0, u0, jnp.zeros_like(u0))
        second = (ring[1, b].astype(F32) - dot16(low[...], u0)).astype(BF)
        u1 = dot16(linv[1], second).astype(BF)
        u1 = jnp.where(cblk > 1, u1, jnp.zeros_like(u1))
        for k in range(2):
            rblk = k * 16 + row
            new = (work[k, b].astype(F32) - dot16(pan[0, k], u0)).astype(BF)
            new = (new.astype(F32) - dot16(pan[1, k], u1)).astype(BF)
            out[k, b] = new
            if k == 0:
                @pl.when((rblk == 0) & (cblk > 0))
                def _(k=k, b=b):
                    out[k, b] = u0

                @pl.when((rblk == 1) & (cblk > 1))
                def _(k=k, b=b):
                    out[k, b] = u1

            if b == 0:
                for s in range(2):
                    @pl.when((cblk == s) & (rblk > s))
                    def _(k=k, b=b, s=s):
                        out[k, b] = pan[s, k]

                    @pl.when((cblk == s) & (rblk == s))
                    def _(k=k, b=b, s=s):
                        out[k, b] = packed[s]


WIDE = 2


def update(work, ring, linv, low, pan, packed):
    full = lambda *shape: pl.BlockSpec(shape, lambda j: (0,) * len(shape))
    stream = pl.BlockSpec((2, WIDE, NB, NB), lambda j: (0, j, 0, 0))
    return pl.pallas_call(
        bulk,
        grid=(NCOL // WIDE,),
        out_shape=jax.ShapeDtypeStruct(work.shape, BF),
        in_specs=[
            stream, stream, full(2, NB, NB), full(NB, NB), full(2, 2, NB, NB), full(2, NB, NB),
        ],
        out_specs=stream,
        name="bulk",
    )(work, ring, linv, low, pan, packed)


def local(matrix):
    work = matrix.transpose(0, 1, 3, 4, 2, 5).reshape(2, NCOL, NB, NB)
    ring, corner, panel = gather(work)
    linv, low, pan, packed = factors(corner, panel)
    out = update(work, ring, linv, low, pan, packed)
    return out.reshape(2, 1, NCOL, 1, NB, NB).transpose(0, 1, 4, 2, 3, 5)


def solution(mesh):
    spec = P(None, "row", None, None, "col", None)
    return jax.shard_map(local, mesh=mesh, in_specs=(spec,), out_specs=spec, check_vma=False)
```

profile of v0, /device:TPU:1, one launch (start us, length us, event | category | flops | bytes accessed | tf_op | source)
XLA Modules:
  0.0 167.4 jit_solution(16104751653561475200)
XLA Ops:
  0.0 108.7 %gather.1 = (bf16[2,22,256,256]{3,2,1,0:T(8,128)(2,1)}, bf16[2,2,256,256]{3,2,1,0:T(8,128)(2,1)}, bf16[2,2,256,256]{3,2,1,0:T(8,128)(2,1)}) custom-call(bf16[2,22,256,256]{3,2,1,0:T(8,128)(2,1)} %bitcast.10), custom_call_target="tpu_custom_call" | custom-call | tf_op jit(solution)/shard_map/gather/pallas_call | solution.py:282
  108.7 33.3 %factors.1 = (bf16[2,256,256]{2,1,0:T(8,128)(2,1)}, bf16[256,256]{1,0:T(8,128)(2,1)}, bf16[2,2,256,256]{3,2,1,0:T(8,128)(2,1)}, bf16[2,256,256]{2,1,0:T(8,128)(2,1)}) custom-call(bf16[2,2,256,256]{3,2,1,0:T(8,128)(2,1)} %get-tuple-element.13.corner, bf16[2,2,256,256]{3,2,1,0:T(8,128)(2,1)} %get-tuple-element.14.panel), custom_call_target="tpu_custom_call" | custom-call | tf_op jit(solution)/shard_map/factors/pallas_call | solution.py:324
  142.0 25.4 %bulk.1 = bf16[2,22,256,256]{3,2,1,0:T(8,128)(2,1)} custom-call(bf16[2,22,256,256]{3,2,1,0:T(8,128)(2,1)} %bitcast.11, bf16[2,22,256,256]{3,2,1,0:T(8,128)(2,1)} %get-tuple-element.12.ring, bf16[2,256,256]{2,1,0:T(8,128)(2,1)} %get-tuple-element.15.linv, bf16[256,256]{1,0:T(8,128)(2,1)} %get-tuple-element.16.low, ...), custom_call_target="tpu_custom_call" | custom-call | tf_op jit(solution)/shard_map/bulk/pallas_call | solution.py:391
where the time goes:
time: 168 us; the launch traced here: 167 us
  Pallas kernels  167 us (99%)
    pallas_call x1, Pallas kernels, gather(): pl.pallas_call(comm, out_shape=(block((2, NCOL, NB, NB), BF), block((2, 2...  109 us
    pallas_call x1, Pallas kernels, factors(): pl.pallas_call(small, out_shape=(block((2, NB, NB), BF), block((NB, NB),...  33.3 us
    pallas_call x1, Pallas kernels, update(): pl.pallas_call(bulk, grid=(NCOL // WIDE,), out_shape=jax.ShapeDtypeStruct...  25.4 us

commit v1 on v0

v1 whole, which is shorter than its diff:
```python
import functools

import jax
import jax.numpy as jnp
from jax import lax
from jax.experimental import pallas as pl
from jax.experimental.pallas import tpu as pltpu
from jax.sharding import PartitionSpec as P

NB = 256
HB = 128
BF = jnp.bfloat16
F32 = jnp.float32


def dot32(a, b):
    return jnp.dot(a, b, precision=lax.Precision.HIGHEST, preferred_element_type=F32)


def dot16(a, b):
    return jnp.dot(a, b, preferred_element_type=F32)


def pick_lane(x, lane):
    return jnp.take_along_axis(x, jnp.full(x.shape, lane, jnp.int32), axis=1)


def pick_row(x, row):
    return jnp.broadcast_to(x[row : row + 1, :], x.shape)


def eliminate(m, rows, cols):
    lane = lax.broadcasted_iota(jnp.int32, (8, HB), 1)
    sub = lax.broadcasted_iota(jnp.int32, (8, HB), 0)

    def group(g, carry):
        base = pl.multiple_of(g * 8, 8)
        own = m[pl.ds(base, 8), :]
        cb = [pick_lane(own, base + u) for u in range(8)]
        saved_row = jnp.zeros((8, HB), F32)
        saved_col = cols[pl.ds(base, 8), :]
        for t in range(8):
            here = lane == base + t
            at = sub == t
            inv = 1.0 / pick_row(cb[t], t)
            saved_row = jnp.where(at, own, saved_row)
            saved_col = jnp.where(here, jnp.where(at, inv, cb[t] * inv), saved_col)
            mult = jnp.where(at, -1.0, cb[t])
            scaled = jnp.where(here, 1.0, pick_row(own, t)) * inv
            own = jnp.where(here | at, 0.0, own) - mult * scaled
            for u in range(t + 1, 8):
                cb[u] = jnp.where(at, 0.0, cb[u]) - mult * (pick_row(cb[u], t) * inv)
        inside = (lane >= base) & (lane < base + 8)
        wr = [pick_row(own, u) for u in range(8)]
        for r in range(HB // 8):
            part = pl.ds(8 * r, 8)
            old = m[part, :]
            cols[part, :] = jnp.where(inside, old, cols[part, :])
            new = jnp.where(inside, 0.0, old)
            for u in range(8):
                new = new - pick_lane(old, base + u) * wr[u]
            m[part, :] = new
        m[pl.ds(base, 8), :] = own
        rows[pl.ds(base, 8), :] = saved_row
        cols[pl.ds(base, 8), :] = saved_col
        return carry

    lax.fori_loop(0, HB // 8, group, 0)


def pieces(m, rows, cols):
    i = lax.broadcasted_iota(jnp.int32, (HB, HB), 0)
    j = lax.broadcasted_iota(jnp.int32, (HB, HB), 1)
    near = (i // 8) == (j // 8)
    c = cols[...]
    r = rows[...]
    small = jnp.where(near & (i < j), -c, jnp.where(i == j, c, 0.0))
    far = dot32(jnp.where(near, 0.0, c), small)
    mixed = jnp.where(near, c, far)
    low = jnp.where(i > j, mixed, 0.0)
    upinv = jnp.where(i < j, -mixed, jnp.where(i == j, c, 0.0))
    lowinv = jnp.where(i > j, r, jnp.where(i == j, 1.0, 0.0))
    packed = jnp.where(i > j, low, r)
    return m[...], packed, lowinv, upinv


def factor(a, linv, uinv, packed, m, rows, cols, keep):
    lo, hi = pl.ds(0, HB), pl.ds(HB, HB)
    m[...] = a[lo, lo]
    eliminate(m, rows, cols)
    inv, pk, li, ui = pieces(m, rows, cols)
    a12, a21 = a[lo, hi], a[hi, lo]
    w = dot32(inv, a12)
    m[...] = a[hi, hi] - dot32(a21, w)
    keep[0] = w
    keep[1] = dot32(a21, inv)
    packed[lo, lo] = pk.astype(BF)
    packed[lo, hi] = dot32(li, a12).astype(BF)
    packed[hi, lo] = dot32(a21, ui).astype(BF)
    linv[lo, lo] = li.astype(BF)
    uinv[lo, lo] = ui.astype(BF)
    eliminate(m, rows, cols)
    inv, pk, li, ui = pieces(m, rows, cols)
    packed[hi, hi] = pk.astype(BF)
    linv[hi, hi] = li.astype(BF)
    uinv[hi, hi] = ui.astype(BF)
    linv[hi, lo] = (-dot32(li, keep[1])).astype(BF)
    uinv[lo, hi] = (-dot32(keep[0], ui)).astype(BF)
    linv[lo, hi] = jnp.zeros((HB, HB), BF)
    uinv[hi, lo] = jnp.zeros((HB, HB), BF)

MESH = pl.DeviceIdType.MESH
NCOL = 22
PER = 2
NCH = NCOL * PER
CH = NB // PER
NZ = 8
TICKS = 82
PACE = 4


def lag(d):
    return 5 * d


def comm(
    work, ring, q_out, patch,
    rs, rr, ss, sr, kz, kc, ksend, kloc, pr, pt, psend, ploc, loc, fs, fr,
    kb, pb, fb, pk1, pan, a, low, m, rows, cols, part,
):
    row = lax.axis_index("row")
    col = lax.axis_index("col")
    z, core = row // 2, row % 2
    x, y = col // 4, col % 4
    sib = row + 1 - 2 * core

    def pos(xx, yy):
        return ((xx + 4) % 4) * 4 + (yy + 4) % 4

    def rowof(zz, cc):
        return ((zz + NZ) % NZ) * 2 + cc

    def remote(src, dst, send, recv, dev):
        return pltpu.make_async_remote_copy(
            src_ref=src, dst_ref=dst, send_sem=send, recv_sem=recv, device_id=dev, device_id_type=MESH
        )

    barrier = pltpu.get_barrier_semaphore()

    def greet(dev):
        pl.semaphore_signal(barrier, inc=1, device_id=dev, device_id_type=MESH)

    greet((sib, col))

    @pl.when(core == 0)
    def _():
        greet((rowof(z + 1, 0), col))
        greet((rowof(z - 1, 0), col))
        for step in (1, 2, 3):
            greet((row, pos(x, y + step)))
        greet((row, pos(x + 1, y)))
        greet((row, pos(x - 1, y)))

        @pl.when(x == 0)
        def _():
            for xx in (1, 2, 3):
                greet((sib, pos(xx, y)))

        @pl.when((z == 1) | (z == NZ - 1))
        def _():
            greet((rowof(0, 1), col))

        pl.semaphore_wait(
            barrier, 8 + jnp.where(x == 0, 3, 0) + jnp.where((z == 1) | (z == NZ - 1), 1, 0)
        )

    @pl.when(core == 1)
    def _():
        @pl.when(x != 0)
        def _():
            greet((sib, pos(0, y)))

        @pl.when(z == 0)
        def _():
            greet((rowof(1, 0), col))
            greet((rowof(NZ - 1, 0), col))

        pl.semaphore_wait(barrier, 1 + jnp.where(x != 0, 1, 0) + jnp.where(z == 0, 2, 0))

    dist = [z, (NZ - z) % NZ]
    after = [rowof(z + 1, 0), rowof(z - 1, 0)]
    short = col < 2
    first = jnp.where(short, PER, 0)
    extra = jnp.where(short, 2, 0)

    def piece(ref, n):
        return ref.at[n // PER, pl.ds(pl.multiple_of((n % PER) * CH, CH), CH), :]

    def ahead(r, n, src):
        return remote(piece(src, n), piece(ring.at[r], n), rs.at[r, n], rr.at[r, n], (after[r], col))

    def across(r, n, src):
        return remote(piece(src, n), piece(ring.at[r], n), ss.at[r, n], sr.at[r, n], (sib, col))

    mine = work.at[0]
    fill = pltpu.make_async_copy(mine, ring.at[core], loc.at[0])

    def loop(lo, hi, body):
        lax.fori_loop(lo, hi, lambda n, c: (body(n), c)[1], 0)

    def half(ref, h):
        return ref.at[pl.ds(h * HB, HB), :]

    def kpiece(c, s, h):
        return half(kb.at[c, s], h)

    def corner_sends(c, s):
        root = y == s
        return [
            (root & (z < 4) & (((z > 0) if c else (z >= 0))), (rowof(z + 1, 0), col), 0),
            (root & ((z > 5) if c else ((z > 5) | (z == 0))), (rowof(z - 1, 0), col), 0),
            (root, (row, pos(x, y + 2)), 0),
            (root, (row, pos(x, y + 1)), 0),
            (root, (row, pos(x, y + 3)), 0),
            (None, (sib, pos(x + 2, y)), 1),
            (None, (sib, pos(x + 1, y)), 1),
            (None, (sib, pos(x + 3, y)), 1),
            (None, (sib, col), 1),
        ]

    def each(c, s, h, act):
        for slot, (cond, dev, to) in enumerate(corner_sends(c, s)):
            sem = (kc if to else kz).at[c, s, h]
            copy = remote(kpiece(c, s, h), kpiece(c, s, h), ksend.at[c, s, h, slot], sem, dev)
            if cond is None:
                act(copy)
            else:
                pl.when(cond)(functools.partial(act, copy))

    def kwait(c, s, h, sem):
        remote(kpiece(c, s, h), kpiece(c, s, h), ksend.at[c, s, h, 0], sem.at[c, s, h], (row, col)).wait_recv()

    def corner_event(c, s):
        for h in range(2):
            if c == 0:
                @pl.when((z == 0) & (y == s))
                def _():
                    pltpu.make_async_copy(half(mine.at[0], h), kpiece(c, s, h), kloc.at[s, h]).wait()

                @pl.when((z > 0) | (y != s))
                def _():
                    kwait(c, s, h, kz)
            else:
                kwait(c, s, h, kz)
            each(c, s, h, lambda copy: copy.start())

    rel = [(y - s + 4) % 4 for s in range(2)]

    def is_root(s):
        return (x == 0) & (rel[s] == 0)

    def panel_sends(c, s):
        return [
            ((x == 0) & (rel[s] < 2), (row, pos(x, y + 1))),
            ((x == 0) & (rel[s] == 0), (row, pos(x, y - 1))),
            (x < 2, (row, pos(x + 1, y))),
            (x == 0, (row, pos(x - 1, y))),
        ]

    def each_panel(c, s, k, act):
        item = pb.at[c, s, k]
        for slot, (cond, dev) in enumerate(panel_sends(c, s)):
            pl.when(cond)(
                functools.partial(act, remote(item, item, psend.at[c, s, k, slot], pr.at[c, s, k], dev))
            )
        if c == 1:
            pl.when(jnp.logical_not(is_root(s)))(
                functools.partial(act, remote(item, item, psend.at[c, s, k, 4], pt.at[s, k], (sib, col)))
            )

    def own_panel(s, k):
        return pltpu.make_async_copy(work.at[k, 0], pb.at[core, s, k], ploc.at[s, k])

    def panel_event(c, s, k):
        item = pb.at[c, s, k]
        arrive = remote(item, item, psend.at[c, s, k, 0], pr.at[c, s, k], (row, col))
        if c == 0:
            @pl.when(is_root(s))
            def _():
                own_panel(s, k).wait()

            @pl.when(jnp.logical_not(is_root(s)))
            def _():
                arrive.wait_recv()
        else:
            arrive.wait_recv()
        each_panel(c, s, k, lambda copy: copy.start())

    def solve(s, k, block):
        out = dot16(block, fb[4 * s + 1]).astype(BF)
        pan[s, k] = jnp.where(k * 16 + row > s, out, jnp.zeros_like(out))

    def own_factors(c, recv):
        for k in range(2):
            solve(0, k, pb[c, 0, k])
        for k in range(2):
            block = (pb[c, 1, k].astype(F32) - dot16(pan[0, k], fb[3])).astype(BF)
            solve(1, k, block)
            left = dot16(pan[0, k], fb[0]) + dot16(pan[1, k], fb[6])
            right = dot16(pan[1, k], fb[4])
            if k == 0:
                left = jnp.where(row == c, -(fb[0] if c == 0 else fb[6]).astype(F32), left)
                right = jnp.where(row == c, jnp.zeros_like(right) if c == 0 else -fb[4].astype(F32), right)
            q_out[k, :, pl.ds(0, NB)] = left.astype(BF)
            q_out[k, :, pl.ds(NB, NB)] = right.astype(BF)
            if k == 0 and c == 0:
                patch[k] = jnp.where(
                    row == 0,
                    jnp.where(col == 0, fb[2], fb[3]),
                    jnp.where(col == 0, pan[0, k], pan[1, k]),
                )
            elif k == 0:
                patch[k] = jnp.where(
                    (row == 1) & (col != 0), pk1[...], jnp.where(col == 0, pan[0, k], pan[1, k])
                )
            else:
                patch[k] = jnp.where(col == 0, pan[0, k], pan[1, k])

    def give(i):
        return remote(fb.at[i], fb.at[i], fs.at[i], fr.at[i], (sib, col))

    @pl.when(core == 0)
    def _():
        @pl.when((z == 0) & (x == 0) & (y < 2))
        def _():
            for s in range(2):
                for h in range(2):
                    @pl.when(y == s)
                    def _():
                        pltpu.make_async_copy(half(mine.at[0], h), kpiece(0, s, h), kloc.at[s, h]).start()

        for s in range(2):
            @pl.when(is_root(s))
            def _():
                for k in range(2):
                    own_panel(s, k).start()

        @pl.when(z == 0)
        def _():
            fill.start()

        start = lag(jnp.minimum(z, NZ - z))

        def tick(t):
            for c in range(2):
                for s in range(2):
                    when = start + jnp.where(y == s, 2 * c + 1, 3 * c + 6)

                    @pl.when((x == 0) & (t == when))
                    def _():
                        corner_event(c, s)

            for r in range(2):
                n = t - lag(dist[r]) - extra

                @pl.when((dist[r] > 0) & (n >= first) & (n < NCH))
                def _():
                    ahead(r, n, ring.at[r]).wait_recv()

                    @pl.when(dist[r] < NZ - 1)
                    def _():
                        ahead(r, n, ring.at[r]).start()

                    across(r, n, ring.at[r]).start()

            n = t - extra

            @pl.when((z == 0) & (n >= first) & (n < NCH))
            def _():
                ahead(0, n, mine).start()
                across(0, n, mine).start()

                @pl.when(n >= first + PACE)
                def _():
                    ahead(0, n - PACE, mine).wait_send()

            for s in range(2):
                hops = jnp.where(x == 0, 0, jnp.where(x == 2, 4, 3))
                hops = jnp.where(x == 0, jnp.where(rel[s] == 2, 2, jnp.minimum(rel[s], 1)), hops)
                for k in range(2):
                    for c in range(2):
                        @pl.when(t == start + 9 + 4 * hops + 2 * (4 * k + 2 * s + c))
                        def _():
                            panel_event(c, s, k)

        loop(0, TICKS, tick)
        for i in range(7):
            give(i).wait_recv()
        own_factors(0, None)

        for r in range(2):
            @pl.when((dist[r] > 0) & (dist[r] < NZ - 1))
            def _():
                loop(first, NCH, lambda n: ahead(r, n, mine).wait_send())

            @pl.when(dist[r] > 0)
            def _():
                loop(first, NCH, lambda n: across(r, n, mine).wait_send())

        @pl.when(z == 0)
        def _():
            fill.wait()
            loop(NCH - PACE, NCH, lambda n: ahead(0, n, mine).wait_send())
            loop(first, NCH, lambda n: across(0, n, mine).wait_send())
            loop(first, NCH, lambda n: across(1, n, mine).wait_recv())

        @pl.when(x == 0)
        def _():
            for c in range(2):
                for s in range(2):
                    for h in range(2):
                        each(c, s, h, lambda copy: copy.wait_send())

        for c in range(2):
            for s in range(2):
                for k in range(2):
                    each_panel(c, s, k, lambda copy: copy.wait_send())

    @pl.when(core == 1)
    def _():
        def root_sends(s, act):
            for h in range(2):
                for slot, dev in enumerate(((rowof(1, 0), col), (rowof(NZ - 1, 0), col), (sib, col))):
                    act(remote(
                        half(mine.at[0], h), kpiece(1, s, h), ksend.at[1, s, h, slot], kz.at[1, s, h], dev
                    ))

        def panel_give(s, k):
            return remote(work.at[k, 0], pb.at[1, s, k], psend.at[1, s, k, 0], pr.at[1, s, k], (sib, col))

        for s in range(2):
            @pl.when(is_root(s) & (z == 0))
            def _():
                root_sends(s, lambda copy: copy.start())

            @pl.when(is_root(s))
            def _():
                for k in range(2):
                    panel_give(s, k).start()
                    own_panel(s, k).start()

        @pl.when(z == 0)
        def _():
            fill.start()

            def both(n):
                ahead(1, n, mine).start()
                across(1, n, mine).start()

            loop(first, NCH, both)

        for h in range(2):
            kwait(0, 0, h, kc)
        a[...] = kb[0, 0].astype(F32)
        factor(a, fb.at[0], fb.at[1], fb.at[2], m, rows, cols, part)
        for h in range(2):
            kwait(1, 0, h, kc)
            kwait(0, 1, h, kc)
            kwait(1, 1, h, kc)
        low[...] = dot16(kb[1, 0], fb[1]).astype(BF)
        fb[3] = dot16(fb[0], kb[0, 1]).astype(BF)
        for i in range(4):
            give(i).start()
        a[...] = (kb[1, 1].astype(F32) - dot16(low[...], fb[3])).astype(BF).astype(F32)
        factor(a, fb.at[4], fb.at[5], pk1, m, rows, cols, part)
        give(4).start()
        give(5).start()
        mid = dot16(low[...], fb[0]).astype(BF)
        fb[6] = (-dot16(fb[4], mid)).astype(BF)
        give(6).start()
        for s in range(2):
            for k in range(2):
                @pl.when(is_root(s))
                def _():
                    own_panel(s, k).wait()

                @pl.when(jnp.logical_not(is_root(s)))
                def _():
                    item = pb.at[1, s, k]
                    remote(item, item, psend.at[1, s, k, 4], pt.at[s, k], (sib, col)).wait_recv()
        own_factors(1, None)

        for i in range(7):
            give(i).wait_send()
        for s in range(2):
            @pl.when(is_root(s) & (z == 0))
            def _():
                root_sends(s, lambda copy: copy.wait_send())

            @pl.when(is_root(s))
            def _():
                for k in range(2):
                    panel_give(s, k).wait_send()

        loop(first, NCH, lambda n: across(0, n, mine).wait_recv())

        @pl.when(z == 0)
        def _():
            fill.wait()
            loop(first, NCH, lambda n: ahead(1, n, mine).wait_send())
            loop(first, NCH, lambda n: across(1, n, mine).wait_send())

        @pl.when(z > 0)
        def _():
            loop(first, NCH, lambda n: across(1, n, mine).wait_recv())


def gather(work):
    block = jax.ShapeDtypeStruct
    hbm = pl.BlockSpec(memory_space=pl.ANY)
    vm = pl.BlockSpec(memory_space=pltpu.VMEM)
    dma = pltpu.SemaphoreType.DMA
    mem = pltpu.VMEM
    return pl.pallas_call(
        comm,
        out_shape=(
            block((2, NCOL, NB, NB), BF),
            block((2, NB, 2 * NB), BF),
            block((2, NB, NB), BF),
        ),
        in_specs=[pl.BlockSpec(memory_space=pltpu.HBM)],
        out_specs=(hbm, vm, vm),
        scratch_shapes=[
            dma((2, NCH)), dma((2, NCH)), dma((2, NCH)), dma((2, NCH)),
            dma((2, 2, 2)), dma((2, 2, 2)), dma((2, 2, 2, 9)), dma((2, 2)),
            dma((2, 2, 2)), dma((2, 2)), dma((2, 2, 2, 5)), dma((2, 2)),
            dma((1,)), dma((7,)), dma((7,)),
            mem((2, 2, NB, NB), BF),
            mem((2, 2, 2, NB, NB), BF),
            mem((7, NB, NB), BF),
            mem((NB, NB), BF),
            mem((2, 2, NB, NB), BF),
            mem((NB, NB), F32),
            mem((NB, NB), BF),
            mem((HB, HB), F32),
            mem((HB, HB), F32),
            mem((HB, HB), F32),
            mem((2, HB, HB), F32),
        ],
        compiler_params=pltpu.CompilerParams(
            collective_id=0, has_side_effects=True, vmem_limit_bytes=32 << 20
        ),
        name="gather",
    )(work)


WIDE = 2


def bulk(work, ring, q, patch, out):
    row = lax.axis_index("row")
    col = lax.axis_index("col")
    j = pl.program_id(0)
    for b in range(WIDE):
        top, bottom = ring[0, b], ring[1, b]
        for k in range(2):
            change = dot16(q[k, :, :NB], top) + dot16(q[k, :, NB:], bottom)
            base = work[k, b].astype(F32)
            if k == 0:
                base = jnp.where(row < 2, jnp.zeros_like(base), base)
            out[k, b] = (base - change).astype(BF)

    @pl.when((j == 0) & (col < 2))
    def _():
        for k in range(2):
            out[k, 0] = patch[k]


def update(work, ring, q, patch):
    full = lambda *shape: pl.BlockSpec(shape, lambda j: (0,) * len(shape))
    stream = pl.BlockSpec((2, WIDE, NB, NB), lambda j: (0, j, 0, 0))
    return pl.pallas_call(
        bulk,
        grid=(NCOL // WIDE,),
        out_shape=jax.ShapeDtypeStruct(work.shape, BF),
        in_specs=[stream, stream, full(2, NB, 2 * NB), full(2, NB, NB)],
        out_specs=stream,
        compiler_params=pltpu.CompilerParams(vmem_limit_bytes=32 << 20),
        name="bulk",
    )(work, ring, q, patch)


def local(matrix):
    work = matrix.transpose(0, 1, 3, 4, 2, 5).reshape(2, NCOL, NB, NB)
    ring, q, patch = gather(work)
    out = update(work, ring, q, patch)
    return out.reshape(2, 1, NCOL, 1, NB, NB).transpose(0, 1, 4, 2, 3, 5)


def solution(mesh):
    spec = P(None, "row", None, None, "col", None)
    return jax.shard_map(local, mesh=mesh, in_specs=(spec,), out_specs=spec, check_vma=False)
```

time: 168 us -> 86.2 us (0.51)
  the two profiles are of different devices: /device:TPU:1 before, /device:TPU:60 now
where the time goes in v1:
time: 86.2 us; the launch traced here: 86.1 us
  Pallas kernels  83.4 us (97%)
  local copies, waits for them, and re-layouts  2.63 us (3%)
    pallas_call x1, Pallas kernels, gather(): pl.pallas_call(comm, out_shape=(block((2, NCOL, NB, NB), BF), block((2, N...  75.6 us
    pallas_call x1, Pallas kernels, update(): pl.pallas_call(bulk, grid=(NCOL // WIDE,), out_shape=jax.ShapeDtypeStruct...  7.84 us
    unnamed x2, local copies, waits for them, and re-layouts  2.63 us

profile of v1, /device:TPU:60, one launch (start us, length us, event | category | flops | bytes accessed | tf_op | source)
XLA Modules:
  0.0 86.1 jit_solution(3104034855985093623)
XLA Ops:
  0.0 0.0 copy-start
  0.0 2.6 %copy-done = bf16[2,1,256,22,1,256]{5,2,4,3,1,0:T(8,128)(2,1)S(1)} copy-done((bf16[2,1,256,22,1,256]{5,2,4,3,1,0:T(8,128)(2,1)S(1)}, bf16[2,1,256,22,1,256]{5,2,4,3,1,0:T(8,128)(2,1)}, u32[]{:S(2)}) %copy-start) | copy-done | bytes 5767192
  2.6 75.6 %gather.1 = (bf16[2,22,256,256]{3,2,1,0:T(8,128)(2,1)S(1)}, bf16[2,256,512]{2,1,0:T(8,128)(2,1)S(1)}, bf16[2,256,256]{2,1,0:T(8,128)(2,1)S(1)}) custom-call(bf16[2,22,256,256]{3,2,1,0:T(8,128)(2,1)S(1)} %bitcast.10), custom_call_target="tpu_custom_call" | custom-call | tf_op jit(solution)/shard_map/gather/pallas_call | solution.py:524
  78.2 7.8 %bulk.1 = bf16[2,22,256,256]{3,2,1,0:T(8,128)(2,1)} custom-call(bf16[2,22,256,256]{3,2,1,0:T(8,128)(2,1)S(1)} %bitcast.11, bf16[2,22,256,256]{3,2,1,0:T(8,128)(2,1)S(1)} %get-tuple-element.8.ring, bf16[2,256,512]{2,1,0:T(8,128)(2,1)S(1)} %get-tuple-element.9.q, bf16[2,256,256]{2,1,0:T(8,128)(2,1)S(1)} %get-tuple-element.10.patch), custom_call_target="tpu_custom_call" | custom-call | tf_op jit(solution)/shard_map/bulk/pallas_call | solution.py:582
Async XLA Ops:
  0.0 2.6 %copy-start = (bf16[2,1,256,22,1,256]{5,2,4,3,1,0:T(8,128)(2,1)S(1)}, bf16[2,1,256,22,1,256]{5,2,4,3,1,0:T(8,128)(2,1)}, u32[]{:S(2)}) copy-start(bf16[2,1,256,22,1,256]{5,2,4,3,1,0:T(8,128)(2,1)} %param.1) | copy-start | bytes 17301508

commit v2 on v1

--- a/solution.py
+++ b/solution.py
@@ -32,10 +32,17 @@
 def eliminate(m, rows, cols):
     lane = lax.broadcasted_iota(jnp.int32, (8, HB), 1)
     sub = lax.broadcasted_iota(jnp.int32, (8, HB), 0)
+    wide = lax.broadcasted_iota(jnp.int32, (HB, HB), 1)
+    tall = lax.broadcasted_iota(jnp.int32, (HB, HB), 0)
 
     def group(g, carry):
         base = pl.multiple_of(g * 8, 8)
         own = m[pl.ds(base, 8), :]
+        old = m[...]
+        inside = (wide >= base) & (wide < base + 8)
+        taken = jnp.where(inside, old, 0.0)
+        hi = taken.astype(BF)
+        lo = (taken - hi.astype(F32)).astype(BF)
         cb = [pick_lane(own, base + u) for u in range(8)]
         saved_row = jnp.zeros((8, HB), F32)
         saved_col = cols[pl.ds(base, 8), :]
@@ -50,16 +57,15 @@
             own = jnp.where(here | at, 0.0, own) - mult * scaled
             for u in range(t + 1, 8):
                 cb[u] = jnp.where(at, 0.0, cb[u]) - mult * (pick_row(cb[u], t) * inv)
-        inside = (lane >= base) & (lane < base + 8)
-        wr = [pick_row(own, u) for u in range(8)]
-        for r in range(HB // 8):
-            part = pl.ds(8 * r, 8)
-            old = m[part, :]
-            cols[part, :] = jnp.where(inside, old, cols[part, :])
-            new = jnp.where(inside, 0.0, old)
-            for u in range(8):
-                new = new - pick_lane(old, base + u) * wr[u]
-            m[part, :] = new
+        cols[...] = jnp.where(inside, old, cols[...])
+        w = jnp.where((tall >= base) & (tall < base + 8), jnp.concatenate([own] * 16, 0), 0.0)
+        wh = w.astype(BF)
+        wl = (w - wh.astype(F32)).astype(BF)
+        right = jnp.concatenate(
+            [jnp.concatenate([wh, wl], 1), jnp.concatenate([wh, jnp.zeros_like(wl)], 1)], 0
+        )
+        both = dot16(jnp.concatenate([hi, lo], 1), right)
+        m[...] = jnp.where(inside, 0.0, old) - (both[:, :HB] + both[:, HB:])
         m[pl.ds(base, 8), :] = own
         rows[pl.ds(base, 8), :] = saved_row
         cols[pl.ds(base, 8), :] = saved_col
@@ -84,10 +90,12 @@
     return m[...], packed, lowinv, upinv
 
 
-def factor(a, linv, uinv, packed, m, rows, cols, keep):
+def factor(a, linv, uinv, packed, m, rows, cols, keep, between=None):
     lo, hi = pl.ds(0, HB), pl.ds(HB, HB)
     m[...] = a[lo, lo]
     eliminate(m, rows, cols)
+    if between is not None:
+        between()
     inv, pk, li, ui = pieces(m, rows, cols)
     a12, a21 = a[lo, hi], a[hi, lo]
     w = dot32(inv, a12)
@@ -115,7 +123,7 @@
 NCH = NCOL * PER
 CH = NB // PER
 NZ = 8
-TICKS = 82
+TICKS = 84
 PACE = 4
 
 
@@ -124,8 +132,8 @@
 
 
 def comm(
-    work, ring, q_out, patch,
-    rs, rr, ss, sr, kz, kc, ksend, kloc, pr, pt, psend, ploc, loc, fs, fr,
+    work, ring, q_out, patch, kept,
+    rs, rr, ss, sr, kc, ksend, kloc, pr, pt, psend, ploc, loc, fs, fr,
     kb, pb, fb, pk1, pan, a, low, m, rows, cols, part,
 ):
     row = lax.axis_index("row")
@@ -152,44 +160,63 @@
 
     greet((sib, col))
 
+    near_root = (z == 1) | (z == NZ - 1)
+    short = col < 2
+
+    def one(cond, count):
+        return jnp.where(cond, count, 0)
+
     @pl.when(core == 0)
     def _():
         greet((rowof(z + 1, 0), col))
         greet((rowof(z - 1, 0), col))
-        for step in (1, 2, 3):
+        for step in (1, -1):
             greet((row, pos(x, y + step)))
-        greet((row, pos(x + 1, y)))
-        greet((row, pos(x - 1, y)))
-
-        @pl.when(x == 0)
-        def _():
-            for xx in (1, 2, 3):
-                greet((sib, pos(xx, y)))
-
-        @pl.when((z == 1) | (z == NZ - 1))
+            greet((row, pos(x + step, y)))
+
+        @pl.when((z == 0) & short)
+        def _():
+            greet((rowof(1, 1), col))
+            greet((rowof(NZ - 1, 1), col))
+
+        @pl.when(z == NZ - 1)
         def _():
             greet((rowof(0, 1), col))
 
-        pl.semaphore_wait(
-            barrier, 8 + jnp.where(x == 0, 3, 0) + jnp.where((z == 1) | (z == NZ - 1), 1, 0)
-        )
+        pl.semaphore_wait(barrier, 7 + one((z == 0) & short, 2) + one(z == NZ - 1, 1))
 
     @pl.when(core == 1)
     def _():
+        @pl.when(short)
+        def _():
+            greet((rowof(z + 1, 1), col))
+            greet((rowof(z - 1, 1), col))
+
+            @pl.when(near_root)
+            def _():
+                greet((rowof(0, 0), col))
+
+        @pl.when(x == 0)
+        def _():
+            for step in (1, 2, 3):
+                greet((row, pos(x, y + step)))
+                greet((row, pos(x + step, y)))
+
         @pl.when(x != 0)
         def _():
-            greet((sib, pos(0, y)))
+            greet((row, pos(0, y)))
 
         @pl.when(z == 0)
         def _():
-            greet((rowof(1, 0), col))
             greet((rowof(NZ - 1, 0), col))
 
-        pl.semaphore_wait(barrier, 1 + jnp.where(x != 0, 1, 0) + jnp.where(z == 0, 2, 0))
+        pl.semaphore_wait(
+            barrier,
+            1 + one(z == 0, 1) + one(short, 2) + one(short & near_root, 1) + jnp.where(x == 0, 6, 1),
+        )
 
     dist = [z, (NZ - z) % NZ]
     after = [rowof(z + 1, 0), rowof(z - 1, 0)]
-    short = col < 2
     first = jnp.where(short, PER, 0)
     extra = jnp.where(short, 2, 0)
 
@@ -204,6 +231,7 @@
 
     mine = work.at[0]
     fill = pltpu.make_async_copy(mine, ring.at[core], loc.at[0])
+    keep = pltpu.make_async_copy(work, kept, loc.at[1])
 
     def loop(lo, hi, body):
         lax.fori_loop(lo, hi, lambda n, c: (body(n), c)[1], 0)
@@ -211,48 +239,66 @@
     def half(ref, h):
         return ref.at[pl.ds(h * HB, HB), :]
 
+    def cuts(c, s):
+        return range(2) if c == 0 and s == 0 else (None,)
+
+    def cut(ref, h):
+        return ref if h is None else half(ref, h)
+
     def kpiece(c, s, h):
-        return half(kb.at[c, s], h)
+        return cut(kb.at[c, s], h)
 
     def corner_sends(c, s):
         root = y == s
+        up, down = (z > 0) & (z < 4), z > 5
         return [
-            (root & (z < 4) & (((z > 0) if c else (z >= 0))), (rowof(z + 1, 0), col), 0),
-            (root & ((z > 5) if c else ((z > 5) | (z == 0))), (rowof(z - 1, 0), col), 0),
-            (root, (row, pos(x, y + 2)), 0),
-            (root, (row, pos(x, y + 1)), 0),
-            (root, (row, pos(x, y + 3)), 0),
-            (None, (sib, pos(x + 2, y)), 1),
-            (None, (sib, pos(x + 1, y)), 1),
-            (None, (sib, pos(x + 3, y)), 1),
-            (None, (sib, col), 1),
+            (root & ((up | (z == 0)) if c else up), (rowof(z + 1, 1), col)),
+            (root & ((down | (z == 0)) if c else down), (rowof(z - 1, 1), col)),
+            (root, (row, pos(x, y + 2))),
+            (root, (row, pos(x, y + 1))),
+            (root, (row, pos(x, y + 3))),
+            (None, (row, pos(x + 2, y))),
+            (None, (row, pos(x + 1, y))),
+            (None, (row, pos(x + 3, y))),
         ]
 
-    def each(c, s, h, act):
-        for slot, (cond, dev, to) in enumerate(corner_sends(c, s)):
-            sem = (kc if to else kz).at[c, s, h]
-            copy = remote(kpiece(c, s, h), kpiece(c, s, h), ksend.at[c, s, h, slot], sem, dev)
-            if cond is None:
-                act(copy)
-            else:
-                pl.when(cond)(functools.partial(act, copy))
-
-    def kwait(c, s, h, sem):
-        remote(kpiece(c, s, h), kpiece(c, s, h), ksend.at[c, s, h, 0], sem.at[c, s, h], (row, col)).wait_recv()
+    def each(c, s, act):
+        @pl.when(x == 0)
+        def _():
+            for h in cuts(c, s):
+                for slot, (cond, dev) in enumerate(corner_sends(c, s)):
+                    copy = remote(
+                        kpiece(c, s, h), kpiece(c, s, h), ksend.at[c, s, h or 0, slot], kc.at[c, s, h or 0], dev
+                    )
+                    if cond is None:
+                        act(copy)
+                    else:
+                        pl.when(cond)(functools.partial(act, copy))
+
+    def first_sends(s, act):
+        for h in cuts(0, s):
+            for slot, dev in enumerate(((rowof(1, 1), col), (rowof(NZ - 1, 1), col), (sib, col))):
+                act(remote(
+                    cut(mine.at[0], h), kpiece(0, s, h), ksend.at[0, s, h or 0, slot], kc.at[0, s, h or 0], dev
+                ))
+
+    def own_corner(s):
+        return pltpu.make_async_copy(mine.at[0], kb.at[1, s], kloc.at[s])
 
     def corner_event(c, s):
-        for h in range(2):
-            if c == 0:
-                @pl.when((z == 0) & (y == s))
-                def _():
-                    pltpu.make_async_copy(half(mine.at[0], h), kpiece(c, s, h), kloc.at[s, h]).wait()
-
-                @pl.when((z > 0) | (y != s))
-                def _():
-                    kwait(c, s, h, kz)
-            else:
-                kwait(c, s, h, kz)
-            each(c, s, h, lambda copy: copy.start())
+        def arrive():
+            for h in cuts(c, s):
+                remote(
+                    kpiece(c, s, h), kpiece(c, s, h), ksend.at[c, s, h or 0, 0], kc.at[c, s, h or 0], (row, col)
+                ).wait_recv()
+
+        if c == 0:
+            arrive()
+        else:
+            here = (z == 0) & (x == 0) & (y == s)
+            pl.when(here)(lambda: own_corner(s).wait())
+            pl.when(jnp.logical_not(here))(arrive)
+        each(c, s, lambda copy: copy.start())
 
     rel = [(y - s + 4) % 4 for s in range(2)]
 
@@ -331,13 +377,10 @@
 
     @pl.when(core == 0)
     def _():
-        @pl.when((z == 0) & (x == 0) & (y < 2))
-        def _():
-            for s in range(2):
-                for h in range(2):
-                    @pl.when(y == s)
-                    def _():
-                        pltpu.make_async_copy(half(mine.at[0], h), kpiece(0, s, h), kloc.at[s, h]).start()
+        for s in range(2):
+            @pl.when(is_root(s) & (z == 0))
+            def _():
+                first_sends(s, lambda copy: copy.start())
 
         for s in range(2):
             @pl.when(is_root(s))
@@ -351,14 +394,18 @@
 
         start = lag(jnp.minimum(z, NZ - z))
 
+        solve_at = jnp.where((z == 1) | (z == NZ - 1), 72, TICKS - 1)
+
         def tick(t):
-            for c in range(2):
-                for s in range(2):
-                    when = start + jnp.where(y == s, 2 * c + 1, 3 * c + 6)
-
-                    @pl.when((x == 0) & (t == when))
-                    def _():
-                        corner_event(c, s)
+            @pl.when(t == 24)
+            def _():
+                keep.start()
+
+            @pl.when(t == solve_at)
+            def _():
+                for i in range(7):
+                    give(i).wait_recv()
+                own_factors(0, None)
 
             for r in range(2):
                 n = t - lag(dist[r]) - extra
@@ -389,14 +436,12 @@
                 hops = jnp.where(x == 0, jnp.where(rel[s] == 2, 2, jnp.minimum(rel[s], 1)), hops)
                 for k in range(2):
                     for c in range(2):
-                        @pl.when(t == start + 9 + 4 * hops + 2 * (4 * k + 2 * s + c))
+                        @pl.when(t == start + 2 + 9 * hops + 2 * (4 * k + 2 * s + c))
                         def _():
                             panel_event(c, s, k)
 
         loop(0, TICKS, tick)
-        for i in range(7):
-            give(i).wait_recv()
-        own_factors(0, None)
+        keep.wait()
 
         for r in range(2):
             @pl.when((dist[r] > 0) & (dist[r] < NZ - 1))
@@ -414,12 +459,10 @@
             loop(first, NCH, lambda n: across(0, n, mine).wait_send())
             loop(first, NCH, lambda n: across(1, n, mine).wait_recv())
 
-        @pl.when(x == 0)
-        def _():
-            for c in range(2):
-                for s in range(2):
-                    for h in range(2):
-                        each(c, s, h, lambda copy: copy.wait_send())
+        for s in range(2):
+            @pl.when(is_root(s) & (z == 0))
+            def _():
+                first_sends(s, lambda copy: copy.wait_send())
 
         for c in range(2):
             for s in range(2):
@@ -428,20 +471,14 @@
 
     @pl.when(core == 1)
     def _():
-        def root_sends(s, act):
-            for h in range(2):
-                for slot, dev in enumerate(((rowof(1, 0), col), (rowof(NZ - 1, 0), col), (sib, col))):
-                    act(remote(
-                        half(mine.at[0], h), kpiece(1, s, h), ksend.at[1, s, h, slot], kz.at[1, s, h], dev
-                    ))
-
         def panel_give(s, k):
             return remote(work.at[k, 0], pb.at[1, s, k], psend.at[1, s, k, 0], pr.at[1, s, k], (sib, col))
 
         for s in range(2):
             @pl.when(is_root(s) & (z == 0))
             def _():
-                root_sends(s, lambda copy: copy.start())
+                own_corner(s).start()
+                corner_event(1, s)
 
             @pl.when(is_root(s))
             def _():
@@ -459,14 +496,17 @@
 
             loop(first, NCH, both)
 
-        for h in range(2):
-            kwait(0, 0, h, kc)
+        def others():
+            for c, s in ((0, 1), (1, 0), (1, 1)):
+                pl.when(jnp.logical_not(is_root(s)))(functools.partial(corner_event, c, s))
+
+        pl.when(is_root(1))(functools.partial(corner_event, 0, 1))
+        pl.when(is_root(1) & (z > 0))(functools.partial(corner_event, 1, 1))
+        corner_event(0, 0)
+        pl.when(is_root(0) & (z > 0))(functools.partial(corner_event, 1, 0))
+        keep.start()
         a[...] = kb[0, 0].astype(F32)
-        factor(a, fb.at[0], fb.at[1], fb.at[2], m, rows, cols, part)
-        for h in range(2):
-            kwait(1, 0, h, kc)
-            kwait(0, 1, h, kc)
-            kwait(1, 1, h, kc)
+        factor(a, fb.at[0], fb.at[1], fb.at[2], m, rows, cols, part, others)
         low[...] = dot16(kb[1, 0], fb[1]).astype(BF)
         fb[3] = dot16(fb[0], kb[0, 1]).astype(BF)
         for i in range(4):
@@ -489,13 +529,13 @@
                     item = pb.at[1, s, k]
                     remote(item, item, psend.at[1, s, k, 4], pt.at[s, k], (sib, col)).wait_recv()
         own_factors(1, None)
+        keep.wait()
 
         for i in range(7):
             give(i).wait_send()
         for s in range(2):
-            @pl.when(is_root(s) & (z == 0))
-            def _():
-                root_sends(s, lambda copy: copy.wait_send())
+            for c in range(2):
+                each(c, s, lambda copy: copy.wait_send())
 
             @pl.when(is_root(s))
             def _():
@@ -527,14 +567,15 @@
             block((2, NCOL, NB, NB), BF),
             block((2, NB, 2 * NB), BF),
             block((2, NB, NB), BF),
+            block((2, NCOL, NB, NB), BF),
         ),
         in_specs=[pl.BlockSpec(memory_space=pltpu.HBM)],
-        out_specs=(hbm, vm, vm),
+        out_specs=(hbm, vm, vm, vm),
         scratch_shapes=[
             dma((2, NCH)), dma((2, NCH)), dma((2, NCH)), dma((2, NCH)),
-            dma((2, 2, 2)), dma((2, 2, 2)), dma((2, 2, 2, 9)), dma((2, 2)),
+            dma((2, 2, 2)), dma((2, 2, 2, 8)), dma((2,)),
             dma((2, 2, 2)), dma((2, 2)), dma((2, 2, 2, 5)), dma((2, 2)),
-            dma((1,)), dma((7,)), dma((7,)),
+            dma((2,)), dma((7,)), dma((7,)),
             mem((2, 2, NB, NB), BF),
             mem((2, 2, 2, NB, NB), BF),
             mem((7, NB, NB), BF),
@@ -548,52 +589,66 @@
             mem((2, HB, HB), F32),
         ],
         compiler_params=pltpu.CompilerParams(
-            collective_id=0, has_side_effects=True, vmem_limit_bytes=32 << 20
+            collective_id=0, has_side_effects=True, vmem_limit_bytes=42 << 20
         ),
         name="gather",
     )(work)
 
 
-WIDE = 2
-
-
-def bulk(work, ring, q, patch, out):
+def bulk(work, ring, q, patch, out, made, sem):
     row = lax.axis_index("row")
     col = lax.axis_index("col")
-    j = pl.program_id(0)
-    for b in range(WIDE):
-        top, bottom = ring[0, b], ring[1, b]
+
+    def leave(k, j):
+        return pltpu.make_async_copy(made.at[k, j], out.at[k, j], sem.at[k, j])
+
+    def block(j):
         for k in range(2):
-            change = dot16(q[k, :, :NB], top) + dot16(q[k, :, NB:], bottom)
-            base = work[k, b].astype(F32)
+            change = dot16(q[k, :, :NB], ring[0, j]) + dot16(q[k, :, NB:], ring[1, j])
+            base = work[k, j].astype(F32)
             if k == 0:
-                base = jnp.where(row < 2, jnp.zeros_like(base), base)
-            out[k, b] = (base - change).astype(BF)
-
-    @pl.when((j == 0) & (col < 2))
+                base = base * factor_of_base
+            made[k, j] = (base - change).astype(BF)
+
+    factor_of_base = jnp.where(row < 2, 0.0, 1.0)
+    block(0)
+
+    @pl.when(col < 2)
     def _():
         for k in range(2):
-            out[k, 0] = patch[k]
+            made[k, 0] = patch[k]
+
+    for j in range(NCOL):
+        if j:
+            block(j)
+        for k in range(2):
+            leave(k, j).start()
+
+    def settle(j, c):
+        for k in range(2):
+            leave(k, j).wait()
+        return c
+
+    lax.fori_loop(0, NCOL, settle, 0)
 
 
 def update(work, ring, q, patch):
-    full = lambda *shape: pl.BlockSpec(shape, lambda j: (0,) * len(shape))
-    stream = pl.BlockSpec((2, WIDE, NB, NB), lambda j: (0, j, 0, 0))
+    vm = pl.BlockSpec(memory_space=pltpu.VMEM)
     return pl.pallas_call(
         bulk,
-        grid=(NCOL // WIDE,),
         out_shape=jax.ShapeDtypeStruct(work.shape, BF),
-        in_specs=[stream, stream, full(2, NB, 2 * NB), full(2, NB, NB)],
-        out_specs=stream,
-        compiler_params=pltpu.CompilerParams(vmem_limit_bytes=32 << 20),
+        in_specs=[vm] * 4,
+        out_specs=pl.BlockSpec(memory_space=pltpu.HBM),
+        scratch_shapes=[pltpu.VMEM(work.shape, BF), pltpu.SemaphoreType.DMA((2, NCOL))],
+        compiler_params=pltpu.CompilerParams(vmem_limit_bytes=12 << 20),
         name="bulk",
     )(work, ring, q, patch)
 
 
 def local(matrix):
     work = matrix.transpose(0, 1, 3, 4, 2, 5).reshape(2, NCOL, NB, NB)
-    ring, q, patch = gather(work)
-    out = update(work, ring, q, patch)
+    ring, q, patch, kept = gather(work)
+    out = update(kept, ring, q, patch)
     return out.reshape(2, 1, NCOL, 1, NB, NB).transpose(0, 1, 4, 2, 3, 5)
 
 

time: 86.2 us -> 75.3 us (0.87)
  the two profiles are of different devices: /device:TPU:60 before, /device:TPU:51 now
where the time goes in v2:
time: 75.3 us; the launch traced here: 75.2 us
  Pallas kernels  75.2 us (100%)
    pallas_call x1, Pallas kernels, gather(): pl.pallas_call(comm, out_shape=(block((2, NCOL, NB, NB), BF), block((2, N...  70.8 us
    pallas_call x1, Pallas kernels, update(): pl.pallas_call(bulk, out_shape=jax.ShapeDtypeStruct(work.shape, BF), in_s...  4.42 us

profile of v2, /device:TPU:51, one launch (start us, length us, event | category | flops | bytes accessed | tf_op | source)
XLA Modules:
  0.0 75.2 jit_solution(6794483883647734157)
XLA Ops:
  0.0 70.8 %gather.1 = (bf16[2,22,256,256]{3,2,1,0:T(8,128)(2,1)S(1)}, bf16[2,256,512]{2,1,0:T(8,128)(2,1)S(1)}, bf16[2,256,256]{2,1,0:T(8,128)(2,1)S(1)}, bf16[2,22,256,256]{3,2,1,0:T(8,128)(2,1)S(1)}) custom-call(bf16[2,22,256,256]{3,2,1,0:T(8,128)(2,1)} %bitcast.10), custom_call_target="tpu_custom_call" | custom-call | tf_op jit(solution)/shard_map/gather/pallas_call | solution.py:564
  70.8 4.4 %bulk.1 = bf16[2,22,256,256]{3,2,1,0:T(8,128)(2,1)} custom-call(bf16[2,22,256,256]{3,2,1,0:T(8,128)(2,1)S(1)} %get-tuple-element.9.work, bf16[2,22,256,256]{3,2,1,0:T(8,128)(2,1)S(1)} %get-tuple-element.10.ring, bf16[2,256,512]{2,1,0:T(8,128)(2,1)S(1)} %get-tuple-element.11.q, bf16[2,256,256]{2,1,0:T(8,128)(2,1)S(1)} %get-tuple-element.12.patch), custom_call_target="tpu_custom_call" | custom-call | tf_op jit(solution)/shard_map/bulk/pallas_call | solution.py:637

commit v3 on v2

--- a/solution.py
+++ b/solution.py
@@ -218,7 +218,7 @@
     dist = [z, (NZ - z) % NZ]
     after = [rowof(z + 1, 0), rowof(z - 1, 0)]
     first = jnp.where(short, PER, 0)
-    extra = jnp.where(short, 2, 0)
+    extra = 0
 
     def piece(ref, n):
         return ref.at[n // PER, pl.ds(pl.multiple_of((n % PER) * CH, CH), CH), :]
@@ -436,7 +436,7 @@
                 hops = jnp.where(x == 0, jnp.where(rel[s] == 2, 2, jnp.minimum(rel[s], 1)), hops)
                 for k in range(2):
                     for c in range(2):
-                        @pl.when(t == start + 2 + 9 * hops + 2 * (4 * k + 2 * s + c))
+                        @pl.when(t == start + 6 + 8 * hops + 2 * (4 * k + 2 * s + c))
                         def _():
                             panel_event(c, s, k)
 

time: 75.3 us -> 74.6 us (level)
  no operation moved by 1% of the time
where the time goes in v3:
time: 74.6 us; the launch traced here: 74.5 us
  Pallas kernels  74.5 us (100%)
    pallas_call x1, Pallas kernels, gather(): pl.pallas_call(comm, out_shape=(block((2, NCOL, NB, NB), BF), block((2, N...  70.1 us
    pallas_call x1, Pallas kernels, update(): pl.pallas_call(bulk, out_shape=jax.ShapeDtypeStruct(work.shape, BF), in_s...  4.42 us

profile of v3, /device:TPU:51, one launch (start us, length us, event | category | flops | bytes accessed | tf_op | source)
XLA Modules:
  0.0 74.5 jit_solution(16294850096892375133)
XLA Ops:
  0.0 70.1 %gather.1 = (bf16[2,22,256,256]{3,2,1,0:T(8,128)(2,1)S(1)}, bf16[2,256,512]{2,1,0:T(8,128)(2,1)S(1)}, bf16[2,256,256]{2,1,0:T(8,128)(2,1)S(1)}, bf16[2,22,256,256]{3,2,1,0:T(8,128)(2,1)S(1)}) custom-call(bf16[2,22,256,256]{3,2,1,0:T(8,128)(2,1)} %bitcast.10), custom_call_target="tpu_custom_call" | custom-call | tf_op jit(solution)/shard_map/gather/pallas_call | solution.py:564
  70.1 4.4 %bulk.1 = bf16[2,22,256,256]{3,2,1,0:T(8,128)(2,1)} custom-call(bf16[2,22,256,256]{3,2,1,0:T(8,128)(2,1)S(1)} %get-tuple-element.9.work, bf16[2,22,256,256]{3,2,1,0:T(8,128)(2,1)S(1)} %get-tuple-element.10.ring, bf16[2,256,512]{2,1,0:T(8,128)(2,1)S(1)} %get-tuple-element.11.q, bf16[2,256,256]{2,1,0:T(8,128)(2,1)S(1)} %get-tuple-element.12.patch), custom_call_target="tpu_custom_call" | custom-call | tf_op jit(solution)/shard_map/bulk/pallas_call | solution.py:637
